TPU v7x, 32 devices: a whole 2x2x4 slice. The times are simulated.
32 devices in a mesh: groups: 2 (over x), mesh: 16 (over z, y, core).
Axes of the slice: x: 2, y: 2, z: 4, core: 2. Of those that a mesh axis runs over, the one named last changes fastest.
Arguments:
- elem_count: int32 [32], P('groups'), parts along dimension 0, may hold values from 1 to 12, 96 in all
- elem_nodes: int32 [384, 8], P(('groups', 'mesh')), parts along dimension 0, may hold values from 0 to 143, as said below
- bmat: bfloat16 [384, 1152], P(('groups', 'mesh')), parts along dimension 0, may hold values from -4 to 4
- quad_weight: float32 [384, 8], P(('groups', 'mesh')), parts along dimension 0, may hold values from 0.5 to 2
- displacement: float32 [3, 3072], P(None, ('groups', 'mesh')), parts along dimension 1, may hold values from -6 to 6
- load: float32 [3, 3072], P(None, ('groups', 'mesh')), parts along dimension 1, may hold values from -6 to 6
- eps_old: bfloat16 [3072, 6], P(('groups', 'mesh')), parts along dimension 0, may hold values from -5 to 5
- params: bfloat16 [3072, 32], P(('groups', 'mesh')), parts along dimension 0, may hold values from -1 to 1
- hidden: bfloat16 [3072, 512], P(('groups', 'mesh')), parts along dimension 0, may hold values from -0.8984375 to 0.8984375
- sens: bfloat16 [3072, 16384], P(('groups', 'mesh')), parts along dimension 0, may hold values from -4 to 4
- w_x: float32 [38, 1536], replicated, may hold values from -1 to 1
- w_h: bfloat16 [512, 1536], replicated, may hold values from -0.25 to 0.25
- b_x: float32 [1536], replicated, may hold values from -3 to 3
- b_h: float32 [1536], replicated, may hold values from -3 to 3
- w_out: float32 [512, 6], replicated, may hold values from -0.5 to 0.5
- b_out: float32 [6], replicated, may hold values from -3 to 3
Outputs:
- residual: float32 [3, 3072], P(None, ('groups', 'mesh')), parts along dimension 1
- stiffness: float32 [384, 576], P(('groups', 'mesh')), parts along dimension 0
- force_sens: float32 [384, 768], P(('groups', 'mesh')), parts along dimension 0
- hidden_next: bfloat16 [3072, 512], P(('groups', 'mesh')), parts along dimension 0
- sens_next: bfloat16 [3072, 16384], P(('groups', 'mesh')), parts along dimension 0
There are 2 independent parts, one for each index of `groups`. A program takes and returns all parts, laid end to end along the dimension named above; an argument that names none is the same for every part. Nothing has to cross between parts.
Inputs may be any that keep to these rules, and one draw needn't show every extreme that they name: `elem_count`: live elements are the first rows of their partition; the counts sum to 96, and some partition is full. `elem_nodes`: positions index a window of 24 nodes of the previous partition, its own 96 nodes, and 24 nodes of the next; every partition uses the window's first and last position.
All inputs are finite; a program needn't handle non-finite values.
Results may differ from a plain program's by a relative error of at most 0.0057.
Values may be sent and summed in bfloat16 or wider, within the bound.
A program may use at most 128 MiB of HBM per device.

v0:
```python
import jax
import jax.numpy as jnp
from jax import lax
from jax.sharding import PartitionSpec as P

NSUB = 2


HIGHEST = lax.Precision.HIGHEST


def extended(x, sides, width):
    for axis, dim in sides:
        devices, length = (lax.axis_size(axis), x.shape[dim])
        up = [(i, (i + 1) % devices) for i in range(devices - 1)]
        down = [(j, i) for i, j in up]
        last = lax.slice_in_dim(x, length - width, length, axis=dim)
        first = lax.slice_in_dim(x, 0, width, axis=dim)
        before = lax.ppermute(last, axis, up)
        after = lax.ppermute(first, axis, down)
        x = jnp.concatenate([before, x, after], axis=dim)
    return x


def passed_along(block, axis, distance):
    devices = range(lax.axis_size(axis))
    route = [(i - distance, i) for i in devices if i - distance in devices]
    return lax.ppermute(block, axis, route)


def advance(small_block, hidden_block, sens_block, weights):
    w_x, w_h, b_x, b_h, w_out, b_out = weights
    row_count = hidden_block.shape[0]
    width = hidden_block.shape[1]
    param_count = sens_block.shape[1] // width
    strain_count = (small_block.shape[1] - param_count) // 2
    column_count = strain_count + param_count
    floats = small_block.astype(jnp.float32)
    strain_old = floats[:, :strain_count]
    strain_new = floats[:, strain_count : 2 * strain_count]
    material = floats[:, 2 * strain_count :]
    tangent = jnp.concatenate(
        [
            jnp.zeros((row_count, strain_count, width), jnp.bfloat16),
            sens_block.reshape(row_count, param_count, width),
        ],
        axis=1,
    )
    state = hidden_block
    for substep in range(NSUB):
        fraction = (substep + 1.0) / NSUB
        drive = jnp.concatenate(
            [strain_old + fraction * (strain_new - strain_old), material], axis=1
        )
        input_gates = jnp.dot(drive, w_x, precision=HIGHEST) + b_x
        column_scale = jnp.concatenate(
            [
                jnp.full((strain_count,), fraction, jnp.float32),
                jnp.ones((param_count,), jnp.float32),
            ]
        )
        input_rates = w_x * column_scale[:, None]
        stacked = jnp.concatenate([state[:, None, :], tangent], axis=1)
        product = jnp.dot(
            stacked.reshape(row_count * (column_count + 1), width),
            w_h,
            preferred_element_type=jnp.float32,
        ).reshape(row_count, column_count + 1, 3 * width)
        hidden_gates = product[:, 0, :] + b_h
        hidden_rates = product[:, 1:, :]
        reset = jax.nn.sigmoid(input_gates[:, :width] + hidden_gates[:, :width])
        update = jax.nn.sigmoid(
            input_gates[:, width : 2 * width] + hidden_gates[:, width : 2 * width]
        )
        hidden_cand = hidden_gates[:, 2 * width :]
        candidate = jnp.tanh(input_gates[:, 2 * width :] + reset * hidden_cand)
        previous = state.astype(jnp.float32)
        prev_rates = tangent.astype(jnp.float32)
        reset_rate = (reset * (1.0 - reset))[:, None, :] * (
            input_rates[None, :, :width] + hidden_rates[:, :, :width]
        )
        update_rate = (update * (1.0 - update))[:, None, :] * (
            input_rates[None, :, width : 2 * width] + hidden_rates[:, :, width : 2 * width]
        )
        cand_rate = (1.0 - candidate * candidate)[:, None, :] * (
            input_rates[None, :, 2 * width :]
            + reset_rate * hidden_cand[:, None, :]
            + reset[:, None, :] * hidden_rates[:, :, 2 * width :]
        )
        next_state = (1.0 - update) * candidate + update * previous
        next_rates = (
            (1.0 - update)[:, None, :] * cand_rate
            + update_rate * (previous - candidate)[:, None, :]
            + update[:, None, :] * prev_rates
        )
        state = next_state.astype(jnp.bfloat16)
        tangent = next_rates.astype(jnp.bfloat16)
    final_state = state.astype(jnp.float32)
    final_rates = tangent.astype(jnp.float32)
    stress = jnp.dot(final_state, w_out, precision=HIGHEST) + b_out
    stress_rates = jnp.einsum("rch,hk->rck", final_rates, w_out, precision=HIGHEST)
    micro_out = jnp.concatenate(
        [stress, stress_rates.reshape(row_count, column_count * strain_count)], axis=1
    ).astype(jnp.bfloat16)
    return (state, tangent[:, strain_count:, :].reshape(row_count, param_count * width), micro_out)


def advance_rows(small, hidden, sens, weights):
    row_count = hidden.shape[0]
    blocks = row_count // 8

    def advance_block(pieces):
        return advance(pieces[0], pieces[1], pieces[2], weights)

    results = lax.map(
        advance_block,
        (
            small.reshape(blocks, 8, small.shape[1]),
            hidden.reshape(blocks, 8, hidden.shape[1]),
            sens.reshape(blocks, 8, sens.shape[1]),
        ),
    )
    return tuple((piece.reshape(row_count, piece.shape[2]) for piece in results))


def element_terms(shape_grads, weight, stress, tangent):
    strain_count = stress.shape[2]
    elem_total = stress.shape[0]
    weighted = stress * weight[:, :, None]
    force = jnp.einsum("eqkac,eqk->eac", shape_grads, weighted, precision=HIGHEST)
    strain_rates = tangent[:, :, :strain_count, :] * weight[:, :, None, None]
    left_part = jnp.einsum("eqkac,eqik->eqaci", shape_grads, strain_rates, precision=HIGHEST)
    stiffness = jnp.einsum("eqaci,eqibf->eacbf", left_part, shape_grads, precision=HIGHEST).reshape(
        elem_total, -1
    )
    param_rates = tangent[:, :, strain_count:, :] * weight[:, :, None, None]
    force_sens = jnp.einsum(
        "eqkac,eqjk->eacj", shape_grads, param_rates, precision=HIGHEST
    ).reshape(elem_total, -1)
    return (force, stiffness, force_sens)


def on_device(
    elem_count,
    elem_nodes,
    bmat,
    quad_weight,
    displacement,
    load,
    eps_old,
    params,
    hidden,
    sens,
    w_x,
    w_h,
    b_x,
    b_h,
    w_out,
    b_out,
):
    weights = (w_x, w_h, b_x, b_h, w_out, b_out)
    peer_count = lax.axis_size("mesh")
    my_index = lax.axis_index("mesh")
    elem_cap = elem_nodes.shape[0]
    node_each = elem_nodes.shape[1]
    quad_count = quad_weight.shape[1]
    strain_count = eps_old.shape[1]
    point_cap = quad_count * elem_cap
    point_counts = elem_count * quad_count
    starts = jnp.cumsum(point_counts) - point_counts
    own_start = jnp.take(starts, my_index)
    own_points = jnp.take(point_counts, my_index)
    own_elems = jnp.take(elem_count, my_index)
    node_owned = displacement.shape[1]
    halo_width = node_owned // 4
    widened = extended(displacement, (("mesh", 1),), halo_width)
    node_values = widened[:, elem_nodes]
    shape_grads = bmat.astype(jnp.float32).reshape(elem_cap, quad_count, strain_count, node_each, 3)
    strain = (
        jnp.einsum("eqkac,cea->eqk", shape_grads, node_values, precision=HIGHEST)
        .reshape(point_cap, strain_count)
        .astype(jnp.bfloat16)
    )
    small = jnp.concatenate([eps_old, strain, params], axis=1)
    local_index = jnp.arange(point_cap, dtype=jnp.int32)
    live_point = local_index < own_points
    targets = jnp.arange(peer_count, dtype=jnp.int32)[:, None]
    batch_rows = quad_count * (elem_cap // 2)
    slot_count = -(-point_cap // peer_count)
    columns = jnp.arange(slot_count, dtype=jnp.int32)[None, :]
    local_pick = jnp.mod(targets - own_start, peer_count) + columns * peer_count
    send_ok = local_pick < own_points
    local_pick = jnp.where(send_ok, local_pick, 0)

    def pack_send(values):
        return jnp.where(send_ok[:, :, None], values[local_pick], jnp.zeros((), values.dtype))

    arrived = (
        lax.all_to_all(pack_send(small), "mesh", split_axis=0, concat_axis=0, tiled=True),
        lax.all_to_all(pack_send(hidden), "mesh", split_axis=0, concat_axis=0, tiled=True),
        lax.all_to_all(pack_send(sens), "mesh", split_axis=0, concat_axis=0, tiled=True),
    )
    positions = jnp.arange(batch_rows, dtype=jnp.int32) * peer_count + my_index
    source = jnp.sum((starts[None, :] <= positions[:, None]).astype(jnp.int32), axis=1) - 1
    source_slot = source * slot_count + (positions - starts[source]) // peer_count
    gathered = [
        piece.reshape(peer_count * slot_count, piece.shape[2])[source_slot] for piece in arrived
    ]
    results = advance_rows(gathered[0], gathered[1], gathered[2], weights)
    owner_start = starts[targets]
    back_pick = jnp.mod(my_index - owner_start, peer_count) + columns * peer_count
    back_ok = back_pick < point_counts[targets]
    back_row = jnp.clip((owner_start + back_pick - my_index) // peer_count, 0, batch_rows - 1)

    def pack_back(values):
        return jnp.where(back_ok[:, :, None], values[back_row], jnp.zeros((), values.dtype))

    returned = (
        lax.all_to_all(pack_back(results[0]), "mesh", split_axis=0, concat_axis=0, tiled=True),
        lax.all_to_all(pack_back(results[1]), "mesh", split_axis=0, concat_axis=0, tiled=True),
        lax.all_to_all(pack_back(results[2]), "mesh", split_axis=0, concat_axis=0, tiled=True),
    )
    from_peer = jnp.mod(own_start + local_index, peer_count)
    from_slot = from_peer * slot_count + local_index // peer_count
    placed = [
        jnp.where(
            live_point[:, None],
            piece.reshape(peer_count * slot_count, piece.shape[2])[from_slot],
            jnp.zeros((), piece.dtype),
        )
        for piece in returned
    ]
    hidden_next, sens_next, micro_out = placed
    micro_floats = micro_out.astype(jnp.float32)
    stress = micro_floats[:, :strain_count].reshape(elem_cap, quad_count, strain_count)
    tangent = micro_floats[:, strain_count:].reshape(elem_cap, quad_count, -1, strain_count)
    force, stiffness, force_sens = element_terms(shape_grads, quad_weight, stress, tangent)
    element_live = jnp.arange(elem_cap, dtype=jnp.int32) < own_elems
    force = jnp.where(element_live[:, None, None], force, 0.0)
    stiffness = jnp.where(element_live[:, None], stiffness, 0.0)
    force_sens = jnp.where(element_live[:, None], force_sens, 0.0)
    node_total = widened.shape[1]
    flat_nodes = elem_nodes.reshape(-1)
    incidence = (flat_nodes[:, None] == jnp.arange(node_total, dtype=jnp.int32)[None, :]).astype(
        jnp.float32
    )
    wide_force = jnp.einsum("pc,pn->cn", force.reshape(-1, 3), incidence, precision=HIGHEST)
    owned = wide_force[:, halo_width : halo_width + node_owned]
    from_right = passed_along(wide_force[:, :halo_width], "mesh", -1)
    from_left = passed_along(wide_force[:, halo_width + node_owned :], "mesh", 1)
    owned = owned.at[:, node_owned - halo_width :].add(from_right)
    owned = owned.at[:, :halo_width].add(from_left)
    residual = load - owned
    return (residual, stiffness, force_sens, hidden_next, sens_next)


def solution(mesh):
    return jax.shard_map(
        on_device,
        mesh=mesh,
        in_specs=(
            P("groups"),
            P(("groups", "mesh"), None),
            P(("groups", "mesh"), None),
            P(("groups", "mesh"), None),
            P(None, ("groups", "mesh")),
            P(None, ("groups", "mesh")),
            P(("groups", "mesh"), None),
            P(("groups", "mesh"), None),
            P(("groups", "mesh"), None),
            P(("groups", "mesh"), None),
            P(),
            P(),
            P(),
            P(),
            P(),
            P(),
        ),
        out_specs=(
            P(None, ("groups", "mesh")),
            P(("groups", "mesh"), None),
            P(("groups", "mesh"), None),
            P(("groups", "mesh"), None),
            P(("groups", "mesh"), None),
        ),
        check_vma=False,
    )
```

profile of v0, /device:TPU:18, one launch (start us, length us, event | category | flops | bytes accessed | tf_op | source)
XLA Modules:
  0.0 464.6 jit_solution(15310649140934109150)
XLA Ops:
  0.7 1.5 fusion.116
  2.2 1.9 collective-permute-start
  4.1 4.5 collective-permute-start.1
  15.5 1.7 copy.95
  17.2 1.3 reshape.734
  19.2 1.4 copy.93
  20.5 1.3 reshape.847
  22.5 1.4 copy.96
  23.9 1.4 copy.97
  25.3 2.3 gather_fusion.6
  27.6 1.6 reshape.878
  29.2 1.4 pad_maximum_fusion.1
  30.5 1.4 copy.94
  32.0 2.1 gather_fusion.2
  34.1 1.5 copy.144
  35.6 1.6 multiply_reduce_fusion.1
  37.2 1.5 copy.119
  38.7 1.5 pad_maximum_fusion
  40.1 2.0 gather_fusion.3
  42.1 1.4 reshape.854
  43.5 1.5 broadcast_select_fusion.8
  44.9 1.5 reshape.980
  46.4 5.3 %all-to-all-start = ((bf16[16,2,132]{2,1,0:T(2,128)(2,1)}), bf16[16,2,132]{2,1,0:T(2,128)(2,1)}, u32[]{:S(2)}, u32[]{:S(2)}) async-start(bf16[16,2,132]{2,1,0:T(2,128)(2,1)} %reshape.980), calls=%async_computation | async-start | bytes 32768 | tf_op jit(solution)/shard_map/all_to_all | solution.py:199
  51.7 1.6 broadcast_select_fusion.5
  53.3 4.2 gather_fusion.8
  57.5 5.0 %reshape.894 = bf16[16,6,16384]{2,1,0:T(8,128)(2,1)} reshape(bf16[96,16384]{1,0:T(8,128)(2,1)} %gather_fusion.8) | data formatting | bytes 6291456 | tf_op jit(solution)/shard_map/gather | solution.py:196
  62.5 6.0 %all-to-all-start.1 = ((bf16[16,6,512]{2,1,0:T(8,128)(2,1)}), bf16[16,6,512]{2,1,0:T(8,128)(2,1)S(1)}, u32[]{:S(2)}, u32[]{:S(2)}) async-start(bf16[16,6,512]{2,1,0:T(8,128)(2,1)} %broadcast_select_fusion.5), calls=%async_computation.1 | async-start | bytes 262144 | tf_op jit(solution)/shard_map/all_to_all | solution.py:200
  68.5 4.7 %broadcast_select_fusion.1 = bf16[16,6,16384]{2,1,0:T(8,128)(2,1)} fusion(bf16[16,6,16384]{2,1,0:T(8,128)(2,1)} %reshape.894, pred[16,6]{1,0:T(8,128)(4,1)S(1)} %get-tuple-element.208), kind=kLoop, calls=%fused_computation.129 | loop fusion | flops 1572864 | bytes 6291552 | tf_op jit(solution)/shard_map/jit(_where)/select_n | solution.py:196
  74.1 6.8 %all-to-all-start.2 = ((bf16[16,6,16384]{2,1,0:T(8,128)(2,1)}), bf16[16,6,16384]{2,1,0:T(8,128)(2,1)}, u32[]{:S(2)}, u32[]{:S(2)}) async-start(bf16[16,6,16384]{2,1,0:T(8,128)(2,1)} %broadcast_select_fusion.1), calls=%async_computation.2 | async-start | bytes 8388608 | tf_op jit(solution)/shard_map/all_to_all | solution.py:201
  84.6 1.3 gather_fusion.7
  85.9 87.7 %all-to-all-done.2 = bf16[16,6,16384]{2,1,0:T(8,128)(2,1)} async-done(((bf16[16,6,16384]{2,1,0:T(8,128)(2,1)}), bf16[16,6,16384]{2,1,0:T(8,128)(2,1)}, u32[]{:S(2)}, u32[]{:S(2)}) %all-to-all-start.2) | async-done | bytes 3145760 | tf_op jit(solution)/shard_map/all_to_all | solution.py:201
  173.6 4.9 %reshape.739 = bf16[96,16384]{1,0:T(8,128)(2,1)} reshape(bf16[16,6,16384]{2,1,0:T(8,128)(2,1)} %all-to-all-done.2) | data formatting | bytes 6291456 | tf_op jit(solution)/shard_map/reshape | solution.py:207
  178.4 6.5 %gather_fusion.9 = bf16[48,16384]{1,0:T(8,128)(2,1)} fusion(bf16[96,16384]{1,0:T(8,128)(2,1)} %reshape.739, s32[1024]{0:T(1024)S(1)} %pad_clamp_fusion.2), kind=kCustom, calls=%fused_computation.9 | custom fusion | bytes 3145920 | tf_op jit(solution)/shard_map/gather | solution.py:207
  185.0 129.6 %while.19 = (s32[]{:T(128)}, bf16[6,8,512]{2,1,0:T(8,128)(2,1)S(1)}, bf16[6,8,16384]{2,1,0:T(8,128)(2,1)S(1)}, bf16[6,8,234]{2,1,0:T(8,128)(2,1)S(1)}, bf16[6,8,...) while((s32[]{:T(128)}, ...), condition=%wide.region_3.4_spmd, body=%wide.region_2.3_spmd.sunk | while | flops 1011072320 | bytes 20770736 | solution.py:115
  202.1 1.7 slice.439
  203.8 1.8 broadcast_in_dim.293
  223.7 1.7 slice.439
  225.4 1.8 broadcast_in_dim.293
  245.3 1.7 slice.439
  247.0 1.8 broadcast_in_dim.293
  266.9 1.7 slice.439
  268.6 1.8 broadcast_in_dim.293
  288.4 1.7 slice.439
  290.2 1.8 broadcast_in_dim.293
  310.0 1.7 slice.439
  311.8 1.8 broadcast_in_dim.293
  315.5 1.4 broadcast_select_fusion.7
  316.9 4.7 %all-to-all-start.3 = ((bf16[16,6,234]{2,1,0:T(8,128)(2,1)}), bf16[16,6,234]{2,1,0:T(8,128)(2,1)S(1)}, u32[]{:S(2)}, u32[]{:S(2)}) async-start(bf16[16,6,234]{2,1,0:T(8,128)(2,1)} %broadcast_select_fusion.7), calls=%async_computation.3 | async-start | bytes 131072 | tf_op jit(solution)/shard_map/all_to_all | solution.py:221
  323.3 4.2 gather_fusion.14
  327.5 5.0 %reshape.942 = bf16[16,6,16384]{2,1,0:T(8,128)(2,1)} reshape(bf16[96,16384]{1,0:T(8,128)(2,1)} %gather_fusion.14) | data formatting | bytes 6291456 | tf_op jit(solution)/shard_map/gather | solution.py:216
  332.5 6.0 %all-to-all-start.4 = ((bf16[16,6,512]{2,1,0:T(8,128)(2,1)}), bf16[16,6,512]{2,1,0:T(8,128)(2,1)S(1)}, u32[]{:S(2)}, u32[]{:S(2)}) async-start(bf16[16,6,512]{2,1,0:T(8,128)(2,1)} %broadcast_select_fusion.4), calls=%async_computation.4 | async-start | bytes 262144 | tf_op jit(solution)/shard_map/all_to_all | solution.py:219
  338.5 4.7 %broadcast_select_fusion = bf16[16,6,16384]{2,1,0:T(8,128)(2,1)} fusion(bf16[16,6,16384]{2,1,0:T(8,128)(2,1)} %reshape.942, pred[16,6]{1,0:T(8,128)(4,1)S(1)} %copy-done.16), kind=kLoop, calls=%fused_computation.128 | loop fusion | flops 1572864 | bytes 6291552 | tf_op jit(solution)/shard_map/jit(_where)/select_n | solution.py:216
  344.7 6.8 %all-to-all-start.5 = ((bf16[16,6,16384]{2,1,0:T(8,128)(2,1)}), bf16[16,6,16384]{2,1,0:T(8,128)(2,1)}, u32[]{:S(2)}, u32[]{:S(2)}) async-start(bf16[16,6,16384]{2,1,0:T(8,128)(2,1)} %broadcast_select_fusion), calls=%async_computation.5 | async-start | bytes 8388608 | tf_op jit(solution)/shard_map/all_to_all | solution.py:220
  351.5 1.6 copy.103
  353.8 1.9 copy.109
  355.9 2.4 copy.130
  364.3 2.7 convolution_bitcast_fusion.1
  368.6 1.4 fusion.78
  371.2 3.1 collective-permute-start.2
  375.9 2.2 collective-permute-start.3
  378.1 64.3 %collective-permute-done.2 = f32[3,24]{1,0:T(4,128)S(1)} collective-permute-done((f32[3,24]{1,0:T(4,128)S(1)}, f32[3,24]{1,0:T(4,128)S(1)}, u32[]{:S(2)}, u32[]{:S(2)}) %collective-permute-start.2) | collective-permute-done | bytes 320 | tf_op jit(solution)/shard_map/ppermute | solution.py:28
  446.6 4.9 %reshape.751 = bf16[96,16384]{1,0:T(8,128)(2,1)} reshape(bf16[16,6,16384]{2,1,0:T(8,128)(2,1)} %all-to-all-done.5) | data formatting | bytes 6291456 | tf_op jit(solution)/shard_map/reshape | solution.py:228
  451.5 9.3 %gather_fusion.15 = bf16[96,16384]{1,0:T(8,128)(2,1)} fusion(bf16[96,16384]{1,0:T(8,128)(2,1)} %reshape.751, s32[1024]{0:T(1024)S(1)} %pad_clamp_fusion), kind=kCustom, calls=%fused_computation.15 | custom fusion | bytes 6291840 | tf_op jit(solution)/shard_map/gather | solution.py:228
  460.8 3.8 broadcast_select_fusion.2
  (413 shorter events, 137.4 us)
Async XLA Ops:
  0.6 52.7 %copy-start = (bf16[96,16384]{1,0:T(8,128)(2,1)S(1)}, bf16[96,16384]{1,0:T(8,128)(2,1)}, u32[]{:S(2)}) copy-start(bf16[96,16384]{1,0:T(8,128)(2,1)} %param.31) | copy-start | bytes 9437188
  0.6 17.9 %copy-start.18 = (s32[12,8]{0,1:T(8,128)S(1)}, s32[12,8]{0,1:T(8,128)}, u32[]{:S(2)}) copy-start(s32[12,8]{0,1:T(8,128)} %param.23) | copy-start | bytes 1156
  2.2 27.0 %collective-permute-start = (f32[3,24]{1,0:T(4,128)}, f32[3,24]{1,0:T(4,128)}, u32[]{:S(2)}, u32[]{:S(2)}) collective-permute-start(f32[3,24]{1,0:T(4,128)} %get-tuple-element.205), channel_id=1, source_target_pairs={{0,1},{1,2},{2,3},{3,4},{4,5},{5,6},{6,7},{7,8},{8,9},{9,10},{10,1... | collective-permute-start | bytes 872 | tf_op jit(solution)/shard_map/ppermute | solution.py:19
  4.1 25.1 %collective-permute-start.1 = (f32[3,24]{1,0:T(4,128)}, f32[3,24]{1,0:T(4,128)}, u32[]{:S(2)}, u32[]{:S(2)}) collective-permute-start(f32[3,24]{1,0:T(4,128)} %get-tuple-element.206), channel_id=1, source_target_pairs={{1,0},{2,1},{3,2},{4,3},{5,4},{6,5},{7,6},{8,7},{9,8},{10,9},{11,1... | collective-permute-start | bytes 872 | tf_op jit(solution)/shard_map/ppermute | solution.py:20
  18.5 39.0 %copy-start.5 = (bf16[12,8,6,8,3]{0,4,3,2,1:T(4,128)(2,1)}, bf16[12,8,6,8,3]{0,4,3,2,1:T(4,128)(2,1)S(1)}, u32[]{:S(2)}) copy-start(bf16[12,8,6,8,3]{0,4,3,2,1:T(4,128)(2,1)S(1)} %reshape.734) | copy-start | bytes 82948
  46.4 16.1 %all-to-all-start = ((bf16[16,2,132]{2,1,0:T(2,128)(2,1)}), bf16[16,2,132]{2,1,0:T(2,128)(2,1)}, u32[]{:S(2)}, u32[]{:S(2)}) async-start(bf16[16,2,132]{2,1,0:T(2,128)(2,1)} %reshape.980), calls=%async_computation | async-start | bytes 32768 | tf_op jit(solution)/shard_map/all_to_all | solution.py:199
  62.5 11.5 %all-to-all-start.1 = ((bf16[16,6,512]{2,1,0:T(8,128)(2,1)}), bf16[16,6,512]{2,1,0:T(8,128)(2,1)S(1)}, u32[]{:S(2)}, u32[]{:S(2)}) async-start(bf16[16,6,512]{2,1,0:T(8,128)(2,1)} %broadcast_select_fusion.5), calls=%async_computation.1 | async-start | bytes 262144 | tf_op jit(solution)/shard_map/all_to_all | solution.py:200
  73.2 8.6 %copy-start.17 = (s32[16,6,1]{1,0,2:T(8,128)S(1)}, s32[16,6,1]{1,0,2:T(8,128)}, u32[]{:S(2)}) copy-start(s32[16,6,1]{1,0,2:T(8,128)} %get-tuple-element.209) | copy-start | bytes 1156
  74.1 99.5 %all-to-all-start.2 = ((bf16[16,6,16384]{2,1,0:T(8,128)(2,1)}), bf16[16,6,16384]{2,1,0:T(8,128)(2,1)}, u32[]{:S(2)}, u32[]{:S(2)}) async-start(bf16[16,6,16384]{2,1,0:T(8,128)(2,1)} %broadcast_select_fusion.1), calls=%async_computation.2 | async-start | bytes 8388608 | tf_op jit(solution)/shard_map/all_to_all | solution.py:201
  178.4 6.5 %copy-start.2 = (bf16[512,1536]{1,0:T(8,128)(2,1)S(1)}, bf16[512,1536]{1,0:T(8,128)(2,1)}, u32[]{:S(2)}) copy-start(bf16[512,1536]{1,0:T(8,128)(2,1)} %param.33) | copy-start | bytes 4718596
  178.4 6.5 %copy-start.3 = (f32[38,1536]{1,0:T(8,128)S(1)}, f32[38,1536]{1,0:T(8,128)}, u32[]{:S(2)}) copy-start(f32[38,1536]{1,0:T(8,128)} %param.32) | copy-start | bytes 700420
  188.7 2.9 copy-start.20
  194.8 2.0 copy-start.10
  194.9 0.6 copy-start.8
  194.9 1.3 copy-start.7
  196.1 0.7 copy-start.4
  210.3 2.9 copy-start.20
  216.4 2.0 copy-start.10
  216.5 0.6 copy-start.8
  216.5 1.3 copy-start.7
  217.7 0.7 copy-start.4
  231.9 2.9 copy-start.20
  238.0 2.0 copy-start.10
  238.1 0.6 copy-start.8
  238.1 1.3 copy-start.7
  239.3 0.7 copy-start.4
  253.5 2.9 copy-start.20
  259.6 2.0 copy-start.10
  259.7 0.6 copy-start.8
  259.7 1.3 copy-start.7
  260.9 0.7 copy-start.4
  275.0 2.9 copy-start.20
  281.2 2.0 copy-start.10
  281.3 0.6 copy-start.8
  281.3 1.3 copy-start.7
  282.5 0.7 copy-start.4
  296.6 2.9 copy-start.20
  302.8 2.0 copy-start.10
  302.9 0.6 copy-start.8
  302.9 1.3 copy-start.7
  304.1 0.7 copy-start.4
  314.5 8.0 %copy-start.16 = (pred[16,6]{1,0:T(8,128)(4,1)S(1)}, pred[16,6]{1,0:T(8,128)(4,1)}, u32[]{:S(2)}) copy-start(pred[16,6]{1,0:T(8,128)(4,1)} %get-tuple-element.207) | copy-start | bytes 292
  314.5 8.7 %copy-start.15 = (s32[1024]{0:T(1024)S(1)}, s32[1024]{0:T(1024)}, u32[]{:S(2)}) copy-start(s32[1024]{0:T(1024)} %pad_clamp_fusion.1) | copy-start | bytes 12292
  316.9 15.5 %all-to-all-start.3 = ((bf16[16,6,234]{2,1,0:T(8,128)(2,1)}), bf16[16,6,234]{2,1,0:T(8,128)(2,1)S(1)}, u32[]{:S(2)}, u32[]{:S(2)}) async-start(bf16[16,6,234]{2,1,0:T(8,128)(2,1)} %broadcast_select_fusion.7), calls=%async_computation.3 | async-start | bytes 131072 | tf_op jit(solution)/shard_map/all_to_all | solution.py:221
  332.5 11.5 %all-to-all-start.4 = ((bf16[16,6,512]{2,1,0:T(8,128)(2,1)}), bf16[16,6,512]{2,1,0:T(8,128)(2,1)S(1)}, u32[]{:S(2)}, u32[]{:S(2)}) async-start(bf16[16,6,512]{2,1,0:T(8,128)(2,1)} %broadcast_select_fusion.4), calls=%async_computation.4 | async-start | bytes 262144 | tf_op jit(solution)/shard_map/all_to_all | solution.py:219
  343.2 8.3 %copy-start.6 = (bf16[12,8,6,8,3]{0,4,3,2,1:T(4,128)(2,1)S(1)}, bf16[12,8,6,8,3]{0,4,3,2,1:T(4,128)(2,1)}, u32[]{:S(2)}) copy-start(bf16[12,8,6,8,3]{0,4,3,2,1:T(4,128)(2,1)} %copy-done.5) | copy-start | bytes 82948
  343.2 10.0 %copy-start.25 = (s32[16]{0:T(128)S(1)}, s32[16]{0:T(128)}, u32[]{:S(2)}) copy-start(s32[16]{0:T(128)} %param.22) | copy-start | bytes 196
  343.2 12.5 %copy-start.19 = (s32[12,8]{0,1:T(8,128)S(1)}, s32[12,8]{0,1:T(8,128)}, u32[]{:S(2)}) copy-start(s32[12,8]{0,1:T(8,128)} %param.23) | copy-start | bytes 1156
  343.2 12.6 %copy-start.21 = (f32[12,8]{0,1:T(8,128)S(1)}, f32[12,8]{0,1:T(8,128)}, u32[]{:S(2)}) copy-start(f32[12,8]{0,1:T(8,128)} %param.25) | copy-start | bytes 1156
  344.0 0.7 copy-start.13
  344.7 101.9 %all-to-all-start.5 = ((bf16[16,6,16384]{2,1,0:T(8,128)(2,1)}), bf16[16,6,16384]{2,1,0:T(8,128)(2,1)}, u32[]{:S(2)}, u32[]{:S(2)}) async-start(bf16[16,6,16384]{2,1,0:T(8,128)(2,1)} %broadcast_select_fusion), calls=%async_computation.5 | async-start | bytes 8388608 | tf_op jit(solution)/shard_map/all_to_all | solution.py:220
  361.7 0.6 copy-start.11
  367.6 1.0 copy-start.9
  368.6 1.6 copy-start.12
  368.6 2.3 copy-start.23
  368.6 2.3 copy-start.24
  368.6 75.8 %copy-start.22 = (f32[3,96]{1,0:T(4,128)S(1)}, f32[3,96]{1,0:T(4,128)}, u32[]{:S(2)}) copy-start(f32[3,96]{1,0:T(4,128)} %param.27) | copy-start | bytes 3460
  368.6 76.4 %copy-start.14 = (bf16[16,6,512]{2,1,0:T(8,128)(2,1)S(1)}, bf16[16,6,512]{2,1,0:T(8,128)(2,1)}, u32[]{:S(2)}) copy-start(bf16[16,6,512]{2,1,0:T(8,128)(2,1)} %copy-done.13) | copy-start | bytes 294916
  371.2 71.2 %collective-permute-start.2 = (f32[3,24]{1,0:T(4,128)S(1)}, f32[3,24]{1,0:T(4,128)S(1)}, u32[]{:S(2)}, u32[]{:S(2)}) collective-permute-start(f32[3,24]{1,0:T(4,128)S(1)} %get-tuple-element.204), channel_id=1, source_target_pairs={{1,0},{2,1},{3,2},{4,3},{5,4},{6,5},{7,6},{8,7},{9,8},{10,9},{11,1... | collective-permute-start | bytes 872 | tf_op jit(solution)/shard_map/ppermute | solution.py:28
  375.9 67.8 %collective-permute-start.3 = (f32[3,24]{1,0:T(4,128)S(1)}, f32[3,24]{1,0:T(4,128)S(1)}, u32[]{:S(2)}, u32[]{:S(2)}) collective-permute-start(f32[3,24]{1,0:T(4,128)S(1)} %get-tuple-element.203), channel_id=1, source_target_pairs={{0,1},{1,2},{2,3},{3,4},{4,5},{5,6},{6,7},{7,8},{8,9},{9,10},{10,1... | collective-permute-start | bytes 872 | tf_op jit(solution)/shard_map/ppermute | solution.py:28
  451.5 13.2 %copy-start.1 = (bf16[96,16384]{1,0:T(8,128)(2,1)S(1)}, bf16[96,16384]{1,0:T(8,128)(2,1)}, u32[]{:S(2)}) copy-start(bf16[96,16384]{1,0:T(8,128)(2,1)} %param.31) | copy-start | bytes 9437188
where the time goes:
time: 472 us; the launch traced here: 465 us
  waiting for transfers between devices  155 us (33%)
  local copies, waits for them, and re-layouts  149 us (32%)
  other arithmetic  71.8 us (15%)
  starting transfers between devices  47.4 us (10%)
  matrix products  37.8 us (8%)
    all_to_all x1, waiting for transfers between devices, on_device(): lax.all_to_all(pack_send(sens), 'mesh', split_axis=0, concat_axis=0, tile...  87.7 us
    ppermute x2, waiting for transfers between devices, passed_along(): return lax.ppermute(block, axis, route)  65.3 us
    gather x6, local copies, waits for them, and re-layouts, pack_send(): values[local_pick]  16.4 us
    dot_general x12, matrix products, advance(): input_gates = jnp.dot(drive, w_x, precision=HIGHEST) + b_x  11.8 us
    unnamed x52, local copies, waits for them, and re-layouts  11.2 us
    gather x6, local copies, waits for them, and re-layouts, pack_back(): values[back_row]  11.1 us
    gather x3, local copies, waits for them, and re-layouts, on_device(): piece.reshape(peer_count * slot_count, piece.shape[2])[from_slot]  10.9 us
    broadcast_in_dim x6, local copies, waits for them, and re-layouts, advance_rows(): lax.map(advance_block, (small.reshape(blocks, 8, small.shape[1]), hidden....  10.6 us
  transfers between devices with their start and end apart: 10, of which 5 were waited for; matrix products, arithmetic and copies ran while one was open for 17% of the time, Pallas kernels for 0%

commit v1 on v0

v1 whole, which is shorter than its diff:
```python
import jax
import jax.numpy as jnp
import numpy as np
from jax import lax
from jax.experimental import pallas as pl
from jax.experimental.pallas import tpu as pltpu
from jax.sharding import PartitionSpec as P

NSUB = 2
GROUP = 4
HIGHEST = lax.Precision.HIGHEST
BF = jnp.bfloat16
F32 = jnp.float32


def dot(x, y):
    return jnp.dot(x, y, preferred_element_type=F32)


def split(x):
    high = x.astype(BF)
    return high, (x - high.astype(F32)).astype(BF)


def constants(elems, quads, strains, nodes, params):
    span = nodes * 3
    wide = strains * span
    lane = np.arange(wide)
    k, ac = lane // span, lane % span
    a, c = ac // 3, ac % 3
    points = elems * quads
    out = np.arange(span * span)
    left = ac[:, None] == (out // span)[None, :]
    right = ac[:, None] == (out % span)[None, :]
    cols = np.arange(span * params)
    sens = ac[:, None] == (cols // params)[None, :]
    rows = -(-elems // 16) * 16
    total = np.arange(rows)[:, None] == (np.arange(points) // quads)[None, :]
    of_strain = k[:, None] == np.arange(strains)[None, :]
    spread = np.arange(strains)[:, None] == k[None, :]
    direction = np.arange(3)[:, None] == c[None, :]
    force = (np.arange(nodes * 8)[:, None] == (a * 8 + c)[None, :])
    bf = [m.astype(BF) for m in (left, right, sens, total, of_strain, spread, direction, force)]
    ints = [
        a.astype(np.int32)[None, :],
        k.astype(np.int32)[None, :],
        (cols % params).astype(np.int32)[None, :],
    ]
    return [jnp.asarray(m) for m in bf + ints]


def body(
    count_ref, u_ref, nodes_ref, b_ref, qw_ref, eps_ref, par_ref, hid_ref,
    wx_ref, wh_ref, bx_ref, bh_ref, wo_ref, bo_ref,
    left_ref, right_ref, sensm_ref, total_ref, ofk_ref, spread_ref, dir_ref, forcem_ref,
    la_ref, lk_ref, lj_ref,
    sens_ref,
    wide_ref, stiff_ref, fs_ref, hn_ref, sn_ref,
    coef, wrep, wb, d1, d2, rsum, gs, onehot,
):
    step = pl.program_id(0)
    last = pl.num_programs(0) - 1
    points, width = hid_ref.shape
    elems = stiff_ref.shape[0]
    quads = points // elems
    strains = eps_ref.shape[1]
    node_each = nodes_ref.shape[1]
    window = u_ref.shape[0]
    rows16 = total_ref.shape[0]
    param_count = par_ref.shape[1]
    live = count_ref[lax.axis_index("mesh")] * quads
    half = width // 2

    def rates(stacked, columns, sub, rates_of, old_of, put):
        for jt in range(2):
            lo = jt * half
            if stacked is not None:
                pr = dot(stacked, wh_ref[:, lo : lo + half])
                pz = dot(stacked, wh_ref[:, width + lo : width + lo + half])
                pn = dot(stacked, wh_ref[:, 2 * width + lo : 2 * width + lo + half])
            for pt in range(points // 16):
                at = slice(pt * 16, pt * 16 + 16)
                ca, cb, cc, cr, cz = [coef[sub, i, at, lo : lo + half] for i in range(5)]
                for g in range(columns):
                    rows = slice(g * points + pt * 16, g * points + pt * 16 + 16)
                    vr = rates_of(g, lo)
                    vz = rates_of(g, width + lo)
                    vn = rates_of(g, 2 * width + lo)
                    if stacked is None:
                        new = cb * vr + cc * vz + ca * vn
                    else:
                        new = (
                            cb * (vr + pr[rows])
                            + cc * (vz + pz[rows])
                            + ca * (vn + cr * pn[rows])
                            + cz * old_of(g, at, lo).astype(F32)
                        )
                    put(g, at, lo, new)

    def point_terms(stacked, columns):
        t = dot(stacked, wrep[...]).astype(BF).astype(F32)
        return [(t[g * points : (g + 1) * points] * wb[...]).astype(BF) for g in range(columns)]

    @pl.when(step == 0)
    def _():
        alive = lax.broadcasted_iota(jnp.int32, (points, 1), 0) < live
        b = b_ref[...].astype(F32)
        wb[...] = jnp.where(alive, b * qw_ref[...], 0.0)
        wrep[...] = dot(wo_ref[...].astype(BF), spread_ref[...]).astype(BF)
        node = lax.broadcasted_iota(jnp.int32, (points, window), 1)
        for a in range(node_each):
            hit = jnp.where(nodes_ref[:, a : a + 1] == node, 1.0, 0.0)
            onehot[a * points : (a + 1) * points, :] = hit.astype(BF)
        u_high, u_low = split(u_ref[...])
        spread_high = dot(u_high, dir_ref[...]).astype(BF)
        spread_low = dot(u_low, dir_ref[...]).astype(BF)
        values = dot(onehot[...], spread_high) + dot(onehot[...], spread_low)
        mine = jnp.zeros((points, values.shape[1]), F32)
        for a in range(node_each):
            mine += jnp.where(la_ref[...] == a, values[a * points : (a + 1) * points], 0.0)
        high, low = split(b * mine)
        strain = (dot(high, ofk_ref[...]) + dot(low, ofk_ref[...])).astype(BF).astype(F32)
        eps = eps_ref[...].astype(F32)
        material = jnp.dot(
            par_ref[...].astype(F32), wx_ref[strains : strains + param_count, :],
            precision=HIGHEST, preferred_element_type=F32,
        ) + bx_ref[...]
        state = hid_ref[...]
        for sub in range(NSUB):
            fraction = (sub + 1.0) / NSUB
            drive = eps + fraction * (strain - eps)
            gx = material + jnp.dot(
                drive, wx_ref[0:strains, :], precision=HIGHEST, preferred_element_type=F32
            )
            gh = dot(state, wh_ref[...]) + bh_ref[...]
            reset = jax.nn.sigmoid(gx[:, :width] + gh[:, :width])
            update = jax.nn.sigmoid(gx[:, width : 2 * width] + gh[:, width : 2 * width])
            cand_h = gh[:, 2 * width :]
            cand = jnp.tanh(gx[:, 2 * width :] + reset * cand_h)
            previous = state.astype(F32)
            ca = (1.0 - update) * (1.0 - cand * cand)
            coef[sub, 0] = ca
            coef[sub, 1] = ca * cand_h * (reset * (1.0 - reset))
            coef[sub, 2] = (previous - cand) * (update * (1.0 - update))
            coef[sub, 3] = reset
            coef[sub, 4] = update
            state = ((1.0 - update) * cand + update * previous).astype(BF)
        hn_ref[...] = jnp.where(alive, state.astype(F32), 0.0).astype(BF)
        stress = (dot(state, wrep[...]) + dot(bo_ref[...], spread_ref[...].astype(F32)))
        high, low = split(stress.astype(BF).astype(F32) * wb[...])
        dims = (((1,), (1,)), ((), ()))
        by_point = lax.dot_general(forcem_ref[...], high, dims, preferred_element_type=F32)
        by_point += lax.dot_general(forcem_ref[...], low, dims, preferred_element_type=F32)
        high, low = split(by_point)
        wide = jnp.zeros((8, window), F32)
        for a in range(node_each):
            hot = onehot[a * points : (a + 1) * points, :]
            wide += dot(high[a * 8 : a * 8 + 8], hot) + dot(low[a * 8 : a * 8 + 8], hot)
        wide_ref[...] = wide

    def sens_rate(g, lane):
        return wx_ref[pl.ds(strains + step * GROUP + g, 1), lane : lane + half]

    def put_first(g, at, lo, new):
        d1[pl.ds(g * points + at.start, 16), lo : lo + half] = new.astype(BF)

    def put_last(g, at, lo, new):
        d2[pl.ds(g * points + at.start, 16), lo : lo + half] = new.astype(BF)
        alive = lax.broadcasted_iota(jnp.int32, (16, 1), 0) + at.start < live
        sn_ref[at, g * width + lo : g * width + lo + half] = jnp.where(alive, new, 0.0).astype(BF)

    stacked = jnp.concatenate(
        [sens_ref[:, g * width : (g + 1) * width] for g in range(GROUP)], axis=0
    )
    rates(
        stacked, GROUP, 0, sens_rate,
        lambda g, at, lo: sens_ref[at, g * width + lo : g * width + lo + half], put_first,
    )
    many = GROUP * points
    rates(
        d1[0:many, :], GROUP, 1, sens_rate,
        lambda g, at, lo: d1[g * points + at.start : g * points + at.stop, lo : lo + half],
        put_last,
    )
    for g, piece in enumerate(point_terms(d2[0:many, :], GROUP)):
        where = pl.multiple_of((step * GROUP + g) * rows16, rows16)
        rsum[pl.ds(where, rows16), :] = dot(total_ref[...], piece).astype(BF)

    @pl.when(step == last)
    def _():
        def strain_rate(scale):
            return lambda g, lane: wx_ref[g : g + 1, lane : lane + half] * scale

        def put_second(g, at, lo, new):
            d2[pl.ds(g * points + at.start, 16), lo : lo + half] = new.astype(BF)

        some = strains * points
        rates(None, strains, 0, strain_rate(1.0 / NSUB), None, put_first)
        rates(
            d1[0:some, :], strains, 1, strain_rate(1.0),
            lambda g, at, lo: d1[g * points + at.start : g * points + at.stop, lo : lo + half],
            put_second,
        )
        for i, piece in enumerate(point_terms(d2[0:some, :], strains)):
            gs[i * points : (i + 1) * points, :] = piece
        b = b_ref[...].astype(F32)
        acc = jnp.zeros((points, stiff_ref.shape[1]), F32)
        for i in range(strains):
            one = jnp.where(lk_ref[...] == i, b, 0.0).astype(BF)
            acc += dot(gs[i * points : (i + 1) * points, :], left_ref[...]) * dot(
                one, right_ref[...]
            )
        stiff_ref[...] = jnp.sum(acc.reshape(elems, quads, acc.shape[1]), axis=1)
        placed = dot(rsum[...], sensm_ref[...])
        fs = jnp.zeros((rows16, fs_ref.shape[1]), F32)
        for j in range(param_count):
            fs += jnp.where(lj_ref[...] == j, placed[j * rows16 : (j + 1) * rows16], 0.0)
        fs_ref[...] = fs[:elems]


def on_device(
    elem_count, elem_nodes, bmat, quad_weight, displacement, load, eps_old, params,
    hidden, sens, w_x, w_h, b_x, b_h, w_out, b_out,
):
    elems, node_each = elem_nodes.shape
    quads = quad_weight.shape[1]
    points, strains = eps_old.shape
    param_count = params.shape[1]
    width = hidden.shape[1]
    owned = displacement.shape[1]
    halo = owned // 4
    window = owned + 2 * halo
    wide = strains * node_each * 3
    peers = lax.axis_size("mesh")
    up = [(i, i + 1) for i in range(peers - 1)]
    down = [(i + 1, i) for i in range(peers - 1)]
    before = lax.ppermute(displacement[:, owned - halo :], "mesh", up)
    after = lax.ppermute(displacement[:, :halo], "mesh", down)
    u = jnp.concatenate([before, displacement, after], axis=1).T
    nodes = jnp.repeat(elem_nodes, quads, axis=0)
    consts = constants(elems, quads, strains, node_each, param_count)
    rows16 = consts[3].shape[0]
    operands = [
        u, nodes, bmat.reshape(points, wide), quad_weight.reshape(points, 1), eps_old, params,
        hidden, w_x, w_h, b_x[None], b_h[None], w_out, b_out[None], *consts,
    ]
    columns = max(GROUP, strains)

    def whole(x):
        return pl.BlockSpec(x.shape, lambda i: (0, 0))

    def const_out(shape):
        return pl.BlockSpec(shape, lambda i: (0, 0))

    streamed = pl.BlockSpec((points, GROUP * width), lambda i: (0, i))
    span = node_each * 3
    force, stiffness, force_sens, hidden_next, sens_next = pl.pallas_call(
        body,
        grid=(param_count // GROUP,),
        in_specs=[pl.BlockSpec(memory_space=pltpu.SMEM)] + [whole(x) for x in operands] + [streamed],
        out_specs=[
            const_out((8, window)), const_out((elems, span * span)),
            const_out((elems, span * param_count)), const_out((points, width)), streamed,
        ],
        out_shape=[
            jax.ShapeDtypeStruct((8, window), F32),
            jax.ShapeDtypeStruct((elems, span * span), F32),
            jax.ShapeDtypeStruct((elems, span * param_count), F32),
            jax.ShapeDtypeStruct((points, width), BF),
            jax.ShapeDtypeStruct(sens.shape, BF),
        ],
        scratch_shapes=[
            pltpu.VMEM((NSUB, 5, points, width), F32),
            pltpu.VMEM((width, wide), BF),
            pltpu.VMEM((points, wide), F32),
            pltpu.VMEM((columns * points, width), BF),
            pltpu.VMEM((columns * points, width), BF),
            pltpu.VMEM((param_count * rows16, wide), BF),
            pltpu.VMEM((strains * points, wide), BF),
            pltpu.VMEM((node_each * points, window), BF),
        ],
        compiler_params=pltpu.CompilerParams(vmem_limit_bytes=48 << 20),
    )(elem_count, *operands, sens)
    force = force[:3]
    from_right = lax.ppermute(force[:, :halo], "mesh", down)
    from_left = lax.ppermute(force[:, halo + owned :], "mesh", up)
    mid = force[:, halo : halo + owned]
    gap = jnp.zeros((3, owned - halo), F32)
    residual = load - (
        mid
        + jnp.concatenate([gap, from_right], axis=1)
        + jnp.concatenate([from_left, gap], axis=1)
    )
    return (residual, stiffness, force_sens, hidden_next, sens_next)


def solution(mesh):
    both = ("groups", "mesh")
    rows, cols = P(both, None), P(None, both)
    return jax.shard_map(
        on_device,
        mesh=mesh,
        in_specs=(P("groups"), rows, rows, rows, cols, cols) + (rows,) * 4 + (P(),) * 6,
        out_specs=(cols, rows, rows, rows, rows),
        check_vma=False,
    )
```

time: 472 us -> 61.1 us (0.13); the launches traced: 465 us -> 60.1 us
  waiting for transfers between devices: 155 us -> 3.39 us
  local copies, waits for them, and re-layouts: 149 us -> 20.3 us
  other arithmetic: 71.8 us -> 1.41 us
  matrix products: 37.8 us -> 0 us
  starting transfers between devices: 47.4 us -> 10.8 us
  Pallas kernels: 0 us -> 23.4 us
    all_to_all x6 -> x0, waiting for transfers between devices: 89.4 us -> none  [the longest x1 87.7 us: on_device(): lax.all_to_all(pack_send(sens), 'mesh', split_axis=0, concat_axis=0, tile...]
    ppermute x4, waiting for transfers between devices: 65.3 us -> 3.39 us  [the longest x1 3.39 us: on_device(): from_left = lax.ppermute(force[:, halo + owned:], 'mesh', up)]
    gather x22 -> x0, local copies, waits for them, and re-layouts: 51.6 us -> none  [the longest x6 16.4 us: pack_send(): values[local_pick]]
    dot_general x40 -> x0, matrix products: 37.8 us -> none  [the longest x12 11.8 us: advance(): input_gates = jnp.dot(drive, w_x, precision=HIGHEST) + b_x]
    all_to_all x6 -> x0, starting transfers between devices: 35.6 us -> none  [the longest x1 6.82 us: on_device(): lax.all_to_all(pack_send(sens), 'mesh', split_axis=0, concat_axis=0, tile...]
    pallas_call x0 -> x1, Pallas kernels: none -> 23.4 us  [on_device(): pl.pallas_call(body, grid=(param_count // GROUP,), in_specs=[pl.BlockSpec...]
    select_n x16 -> x0, other arithmetic: 21.2 us -> none  [the longest x3 7.77 us: pack_send(): jnp.where(send_ok[:, :, None], values[local_pick], jnp.zeros((), values.d...]
    reshape x13 -> x3, local copies, waits for them, and re-layouts: 18.2 us -> 0.96 us  [the longest x1 0.88 us: on_device(): bmat.reshape(points, wide)]
  transfers between devices with their start and end apart: 10 -> 4, of which waited for: 5 -> 1; matrix products, arithmetic and copies ran while one was open for 17% -> 11% of each run, Pallas kernels for 0% -> 0%
where the time goes in v1:
time: 61.1 us; the launch traced here: 60.1 us
  Pallas kernels  23.4 us (38%)
  local copies, waits for them, and re-layouts  20.3 us (33%)
  starting transfers between devices  10.8 us (18%)
  waiting for transfers between devices  3.39 us (6%)
  other arithmetic  1.41 us (2%)
  between operations  0.75 us (1%)
    pallas_call x1, Pallas kernels, on_device(): pl.pallas_call(body, grid=(param_count // GROUP,), in_specs=[pl.BlockSpec...  23.4 us
    unnamed x39, local copies, waits for them, and re-layouts  16.9 us
    ppermute x1, starting transfers between devices, on_device(): after = lax.ppermute(displacement[:, :halo], 'mesh', down)  4.54 us
    ppermute x1, waiting for transfers between devices, on_device(): from_left = lax.ppermute(force[:, halo + owned:], 'mesh', up)  3.39 us
    ppermute x1, starting transfers between devices, on_device(): from_left = lax.ppermute(force[:, halo + owned:], 'mesh', up)  2.4 us
    ppermute x1, starting transfers between devices, on_device(): from_right = lax.ppermute(force[:, :halo], 'mesh', down)  1.92 us
    ppermute x1, starting transfers between devices, on_device(): before = lax.ppermute(displacement[:, owned - halo:], 'mesh', up)  1.91 us
  transfers between devices with their start and end apart: 4, of which 1 were waited for; matrix products, arithmetic and copies ran while one was open for 11% of the time, Pallas kernels for 0%

profile of v1, /device:TPU:18, one launch (start us, length us, event | category | flops | bytes accessed | tf_op | source)
XLA Modules:
  0.0 60.1 jit_solution(3299157155224883066)
XLA Ops:
  0.6 0.8 %fusion.1 = (f32[3,24]{1,0:T(4,128)S(1)}, f32[3,24]{1,0:T(4,128)S(1)}) fusion(f32[3,96]{1,0:T(4,128)} %param.31), kind=kLoop, calls=%fused_computation.4 | loop fusion | bytes 1152 | tf_op jit(solution)/shard_map/slice | solution.py:237
  1.5 1.9 %collective-permute-start = (f32[3,24]{1,0:T(4,128)S(1)}, f32[3,24]{1,0:T(4,128)S(1)}, u32[]{:S(2)}, u32[]{:S(2)}) collective-permute-start(f32[3,24]{1,0:T(4,128)S(1)} %get-tuple-element.17), channel_id=1, source_target_pairs={{0,1},{1,2},{2,3},{3,4},{4,5},{5,6},{6,7},{7,8},{8,9},{9,10},{10,1... | collective-permute-start | bytes 872 | tf_op jit(solution)/shard_map/ppermute | solution.py:237
  3.4 4.5 %collective-permute-start.1 = (f32[3,24]{1,0:T(4,128)S(1)}, f32[3,24]{1,0:T(4,128)S(1)}, u32[]{:S(2)}, u32[]{:S(2)}) collective-permute-start(f32[3,24]{1,0:T(4,128)S(1)} %get-tuple-element.18), channel_id=1, source_target_pairs={{1,0},{2,1},{3,2},{4,3},{5,4},{6,5},{7,6},{8,7},{9,8},{10,9},{11,1... | collective-permute-start | bytes 872 | tf_op jit(solution)/shard_map/ppermute | solution.py:238
  7.9 0.7 %broadcast_in_dim.14.bx_ref = f32[1,1536]{1,0:T(1,128)S(1)} reshape(f32[1536]{0:T(1024)} %param.39) | data formatting | bytes 12288 | tf_op jit(solution)/shard_map/broadcast_in_dim | solution.py:245
  8.6 0.7 %broadcast_in_dim.15.bh_ref = f32[1,1536]{1,0:T(1,128)S(1)} reshape(f32[1536]{0:T(1024)} %param.40) | data formatting | bytes 12288 | tf_op jit(solution)/shard_map/broadcast_in_dim | solution.py:245
  9.3 0.8 %copy.51 = s32[12,8]{1,0:T(8,128)S(1)} copy(s32[12,8]{0,1:T(8,128)} %param.28) | data formatting | bytes 768 | tf_op args[1]
  10.1 0.8 %copy.52 = f32[12,8]{1,0:T(8,128)S(1)} copy(f32[12,8]{0,1:T(8,128)} %param.30) | data formatting | bytes 768 | tf_op args[3]
  10.9 0.8 %copy.54.eps_ref = bf16[96,6]{1,0:T(8,128)(2,1)S(1)} copy(bf16[96,6]{0,1:T(8,128)(2,1)} %param.33) | data formatting | bytes 2304 | tf_op args[6]
  11.7 0.8 %copy.55.par_ref = bf16[96,32]{1,0:T(8,128)(2,1)S(1)} copy(bf16[96,32]{0,1:T(8,128)(2,1)} %param.34) | data formatting | bytes 12288 | tf_op args[7]
  12.5 0.1 reshape.22.qw_ref
  12.6 0.9 %reshape.20.b_ref = bf16[96,144]{1,0:T(8,128)(2,1)S(1)} reshape(bf16[12,1152]{1,0:T(8,128)(2,1)} %param.29) | data formatting | bytes 55296 | tf_op jit(solution)/shard_map/reshape | solution.py:244
  13.4 0.9 %copy.56.wo_ref = f32[512,6]{1,0:T(8,128)S(1)} copy(f32[512,6]{0,1:T(8,128)} %param.41) | data formatting | bytes 24576 | tf_op args[14]
  14.3 0.0 collective-permute-done
  14.3 0.0 collective-permute-done.1
  14.3 0.8 %pad_maximum_fusion = f32[3,144]{1,0:T(4,128)S(1)} fusion(f32[3,24]{1,0:T(4,128)S(1)} %collective-permute-done.1, f32[3,96]{1,0:T(4,128)} %param.31, f32[3,24]{1,0:T(4,128)S(1)} %collective-permute-done), kind=kLoop, calls=%fused_computation.1 | loop fusion | flops 864 | bytes 3456 | tf_op jit(solution)/shard_map/concatenate | solution.py:239
  15.1 0.1 copy.50
  15.2 0.0 copy-start
  15.2 1.4 %copy-done = bf16[512,1536]{1,0:T(8,128)(2,1)S(1)} copy-done((bf16[512,1536]{1,0:T(8,128)(2,1)S(1)}, bf16[512,1536]{1,0:T(8,128)(2,1)}, u32[]{:S(2)}) %copy-start) | copy-done | bytes 1572888
  16.6 0.0 copy-start.1
  16.6 0.9 %copy-done.1 = f32[38,1536]{1,0:T(8,128)S(1)} copy-done((f32[38,1536]{1,0:T(8,128)S(1)}, f32[38,1536]{1,0:T(8,128)}, u32[]{:S(2)}) %copy-start.1) | copy-done | bytes 233496
  17.6 0.0 copy-start.2
  17.6 0.9 %copy-done.2 = bf16[144,768]{1,0:T(8,128)(2,1)S(1)} copy-done((bf16[144,768]{1,0:T(8,128)(2,1)S(1)}, bf16[144,768]{1,0:T(8,128)(2,1)}, u32[]{:S(2)}) %copy-start.2) | copy-done | bytes 221208
  18.5 0.0 copy-start.3
  18.5 0.9 %copy-done.3 = bf16[144,576]{1,0:T(8,128)(2,1)S(1)} copy-done((bf16[144,576]{1,0:T(8,128)(2,1)S(1)}, bf16[144,576]{1,0:T(8,128)(2,1)}, u32[]{:S(2)}) %copy-start.3) | copy-done | bytes 165912
  19.4 0.0 copy-start.4
  19.4 0.9 %copy-done.4 = bf16[144,576]{1,0:T(8,128)(2,1)S(1)} copy-done((bf16[144,576]{1,0:T(8,128)(2,1)S(1)}, bf16[144,576]{1,0:T(8,128)(2,1)}, u32[]{:S(2)}) %copy-start.4) | copy-done | bytes 165912
  20.4 0.0 copy-start.5
  20.4 0.9 %copy-done.5 = bf16[96,512]{1,0:T(8,128)(2,1)S(1)} copy-done((bf16[96,512]{1,0:T(8,128)(2,1)S(1)}, bf16[96,512]{1,0:T(8,128)(2,1)}, u32[]{:S(2)}) %copy-start.5) | copy-done | bytes 98328
  21.2 0.0 copy-start.6
  21.2 0.8 %copy-done.6 = bf16[144,6]{1,0:T(8,128)(2,1)S(1)} copy-done((bf16[144,6]{1,0:T(8,128)(2,1)S(1)}, bf16[144,6]{1,0:T(8,128)(2,1)}, u32[]{:S(2)}) %copy-start.6) | copy-done | bytes 1752
  22.0 0.0 copy-start.7
  22.0 0.8 %copy-done.7 = bf16[64,144]{1,0:T(8,128)(2,1)S(1)} copy-done((bf16[64,144]{1,0:T(8,128)(2,1)S(1)}, bf16[64,144]{1,0:T(8,128)(2,1)}, u32[]{:S(2)}) %copy-start.7) | copy-done | bytes 18456
  22.8 0.0 copy-start.8
  22.8 0.7 %copy-done.8 = bf16[6,144]{1,0:T(8,128)(2,1)S(1)} copy-done((bf16[6,144]{1,0:T(8,128)(2,1)S(1)}, bf16[6,144]{1,0:T(8,128)(2,1)}, u32[]{:S(2)}) %copy-start.8) | copy-done | bytes 1752
  23.5 0.0 copy-start.9
  23.5 0.7 %copy-done.9 = bf16[16,96]{1,0:T(8,128)(2,1)S(1)} copy-done((bf16[16,96]{1,0:T(8,128)(2,1)S(1)}, bf16[16,96]{1,0:T(8,128)(2,1)}, u32[]{:S(2)}) %copy-start.9) | copy-done | bytes 3096
  24.1 0.0 copy-start.10
  24.1 0.7 %copy-done.10 = s32[1,768]{1,0:T(1,128)S(1)} copy-done((s32[1,768]{1,0:T(1,128)S(1)}, s32[1,768]{1,0:T(1,128)}, u32[]{:S(2)}) %copy-start.10) | copy-done | bytes 3096
  24.8 0.0 copy-start.11
  24.8 0.7 %copy-done.11 = bf16[3,144]{1,0:T(4,128)(2,1)S(1)} copy-done((bf16[3,144]{1,0:T(4,128)(2,1)S(1)}, bf16[3,144]{1,0:T(4,128)(2,1)}, u32[]{:S(2)}) %copy-start.11) | copy-done | bytes 888
  25.5 0.0 copy-start.12
  25.5 0.7 %copy-done.12 = s32[1,144]{1,0:T(1,128)S(1)} copy-done((s32[1,144]{1,0:T(1,128)S(1)}, s32[1,144]{1,0:T(1,128)}, u32[]{:S(2)}) %copy-start.12) | copy-done | bytes 600
  26.2 0.0 copy-start.13
  26.2 0.7 %copy-done.13 = s32[1,144]{1,0:T(1,128)S(1)} copy-done((s32[1,144]{1,0:T(1,128)S(1)}, s32[1,144]{1,0:T(1,128)}, u32[]{:S(2)}) %copy-start.13) | copy-done | bytes 600
  26.9 0.0 copy-start.14
  26.9 0.7 %copy-done.14 = s32[16]{0:T(128)S(1)} copy-done((s32[16]{0:T(128)S(1)}, s32[16]{0:T(128)}, u32[]{:S(2)}) %copy-start.14) | copy-done | bytes 88
  27.5 0.0 copy-start.15
  27.5 0.7 %copy-done.15 = f32[6]{0:T(128)S(1)} copy-done((f32[6]{0:T(128)S(1)}, f32[6]{0:T(128)}, u32[]{:S(2)}) %copy-start.15) | copy-done | bytes 48
  28.2 0.0 copy-start.16
  28.2 23.4 %shard_map.290 = (f32[8,144]{1,0:T(8,128)S(1)}, f32[12,576]{1,0:T(8,128)}, f32[12,768]{1,0:T(8,128)}, bf16[96,512]{1,0:T(8,128)(2,1)}, bf16[96,16384]{1,0:T(8,128)(2,1)}) custom-call(s32[16]{0:T(128)S(1)} %copy-done.14, f32[144,3]{1,0:T(8,128)S(1)} %bitcast.4, s32[96,8]{1,0:T(8,128)S(1)} %broadcast_bitcast_fusion.nodes_ref, ...), custom_call_target="tpu_custom_call" | custom-call | tf_op jit(solution)/shard_map/pallas_call | solution.py:257
  51.6 0.1 fusion
  51.7 1.9 %collective-permute-start.2 = (f32[3,24]{1,0:T(4,128)S(1)}, f32[3,24]{1,0:T(4,128)S(1)}, u32[]{:S(2)}, u32[]{:S(2)}) collective-permute-start(f32[3,24]{1,0:T(4,128)S(1)} %get-tuple-element.15), channel_id=1, source_target_pairs={{1,0},{2,1},{3,2},{4,3},{5,4},{6,5},{7,6},{8,7},{9,8},{10,9},{11,1... | collective-permute-start | bytes 872 | tf_op jit(solution)/shard_map/ppermute | solution.py:285
  53.6 2.4 %collective-permute-start.3 = (f32[3,24]{1,0:T(4,128)S(1)}, f32[3,24]{1,0:T(4,128)S(1)}, u32[]{:S(2)}, u32[]{:S(2)}) collective-permute-start(f32[3,24]{1,0:T(4,128)S(1)} %get-tuple-element.16), channel_id=1, source_target_pairs={{0,1},{1,2},{2,3},{3,4},{4,5},{5,6},{6,7},{7,8},{8,9},{9,10},{10,1... | collective-permute-start | bytes 872 | tf_op jit(solution)/shard_map/ppermute | solution.py:286
  56.0 0.0 collective-permute-done.2
  56.0 3.4 %collective-permute-done.3 = f32[3,24]{1,0:T(4,128)S(1)} collective-permute-done((f32[3,24]{1,0:T(4,128)S(1)}, f32[3,24]{1,0:T(4,128)S(1)}, u32[]{:S(2)}, u32[]{:S(2)}) %collective-permute-start.3) | collective-permute-done | bytes 320 | tf_op jit(solution)/shard_map/ppermute | solution.py:286
  59.4 0.0 copy-done.16
  59.4 0.7 %add_subtract_fusion = f32[3,96]{1,0:T(4,128)} fusion(f32[3,96]{1,0:T(4,128)S(1)} %copy-done.16, f32[3,24]{1,0:T(4,128)S(1)} %collective-permute-done.3, f32[3,24]{1,0:T(4,128)S(1)} %collective-permute-done.2, f32[8,144]{1,0:T(8,128)S(1)} %get-tuple-element.10), kind=kLoop, calls=%fused_computation.2 | loop fusion | flops 864 | bytes 4032 | tf_op jit(solution)/shard_map/sub | solution.py:289
  (1 shorter events, 0.0 us)
Async XLA Ops:
  1.5 12.9 %collective-permute-start = (f32[3,24]{1,0:T(4,128)S(1)}, f32[3,24]{1,0:T(4,128)S(1)}, u32[]{:S(2)}, u32[]{:S(2)}) collective-permute-start(f32[3,24]{1,0:T(4,128)S(1)} %get-tuple-element.17), channel_id=1, source_target_pairs={{0,1},{1,2},{2,3},{3,4},{4,5},{5,6},{6,7},{7,8},{8,9},{9,10},{10,1... | collective-permute-start | bytes 872 | tf_op jit(solution)/shard_map/ppermute | solution.py:237
  3.4 11.0 %collective-permute-start.1 = (f32[3,24]{1,0:T(4,128)S(1)}, f32[3,24]{1,0:T(4,128)S(1)}, u32[]{:S(2)}, u32[]{:S(2)}) collective-permute-start(f32[3,24]{1,0:T(4,128)S(1)} %get-tuple-element.18), channel_id=1, source_target_pairs={{1,0},{2,1},{3,2},{4,3},{5,4},{6,5},{7,6},{8,7},{9,8},{10,9},{11,1... | collective-permute-start | bytes 872 | tf_op jit(solution)/shard_map/ppermute | solution.py:238
  15.2 1.4 %copy-start = (bf16[512,1536]{1,0:T(8,128)(2,1)S(1)}, bf16[512,1536]{1,0:T(8,128)(2,1)}, u32[]{:S(2)}) copy-start(bf16[512,1536]{1,0:T(8,128)(2,1)} %wh_ref.1) | copy-start | bytes 4718596
  16.6 0.9 %copy-start.1 = (f32[38,1536]{1,0:T(8,128)S(1)}, f32[38,1536]{1,0:T(8,128)}, u32[]{:S(2)}) copy-start(f32[38,1536]{1,0:T(8,128)} %wx_ref.1) | copy-start | bytes 700420
  17.6 0.9 %copy-start.2 = (bf16[144,768]{1,0:T(8,128)(2,1)S(1)}, bf16[144,768]{1,0:T(8,128)(2,1)}, u32[]{:S(2)}) copy-start(bf16[144,768]{1,0:T(8,128)(2,1)} %constant.26.clone.sensm_ref) | copy-start | bytes 663556
  18.5 0.9 %copy-start.3 = (bf16[144,576]{1,0:T(8,128)(2,1)S(1)}, bf16[144,576]{1,0:T(8,128)(2,1)}, u32[]{:S(2)}) copy-start(bf16[144,576]{1,0:T(8,128)(2,1)} %constant.25.clone.right_ref) | copy-start | bytes 497668
  19.4 0.9 %copy-start.4 = (bf16[144,576]{1,0:T(8,128)(2,1)S(1)}, bf16[144,576]{1,0:T(8,128)(2,1)}, u32[]{:S(2)}) copy-start(bf16[144,576]{1,0:T(8,128)(2,1)} %constant.24.clone.left_ref) | copy-start | bytes 497668
  20.4 0.9 %copy-start.5 = (bf16[96,512]{1,0:T(8,128)(2,1)S(1)}, bf16[96,512]{1,0:T(8,128)(2,1)}, u32[]{:S(2)}) copy-start(bf16[96,512]{1,0:T(8,128)(2,1)} %hid_ref.1) | copy-start | bytes 294916
  21.2 0.8 %copy-start.6 = (bf16[144,6]{1,0:T(8,128)(2,1)S(1)}, bf16[144,6]{1,0:T(8,128)(2,1)}, u32[]{:S(2)}) copy-start(bf16[144,6]{1,0:T(8,128)(2,1)} %constant.28.clone.ofk_ref) | copy-start | bytes 5188
  22.0 0.8 %copy-start.7 = (bf16[64,144]{1,0:T(8,128)(2,1)S(1)}, bf16[64,144]{1,0:T(8,128)(2,1)}, u32[]{:S(2)}) copy-start(bf16[64,144]{1,0:T(8,128)(2,1)} %constant.31.clone.forcem_ref) | copy-start | bytes 55300
  22.8 0.7 %copy-start.8 = (bf16[6,144]{1,0:T(8,128)(2,1)S(1)}, bf16[6,144]{1,0:T(8,128)(2,1)}, u32[]{:S(2)}) copy-start(bf16[6,144]{1,0:T(8,128)(2,1)} %constant.29.clone.spread_ref) | copy-start | bytes 5188
  23.5 0.7 %copy-start.9 = (bf16[16,96]{1,0:T(8,128)(2,1)S(1)}, bf16[16,96]{1,0:T(8,128)(2,1)}, u32[]{:S(2)}) copy-start(bf16[16,96]{1,0:T(8,128)(2,1)} %constant.27.clone.total_ref) | copy-start | bytes 9220
  24.1 0.7 %copy-start.10 = (s32[1,768]{1,0:T(1,128)S(1)}, s32[1,768]{1,0:T(1,128)}, u32[]{:S(2)}) copy-start(s32[1,768]{1,0:T(1,128)} %constant.34.clone.lj_ref) | copy-start | bytes 9220
  24.8 0.7 %copy-start.11 = (bf16[3,144]{1,0:T(4,128)(2,1)S(1)}, bf16[3,144]{1,0:T(4,128)(2,1)}, u32[]{:S(2)}) copy-start(bf16[3,144]{1,0:T(4,128)(2,1)} %constant.30.clone.dir_ref) | copy-start | bytes 2596
  25.5 0.7 %copy-start.12 = (s32[1,144]{1,0:T(1,128)S(1)}, s32[1,144]{1,0:T(1,128)}, u32[]{:S(2)}) copy-start(s32[1,144]{1,0:T(1,128)} %constant.33.clone.lk_ref) | copy-start | bytes 1732
  26.2 0.7 %copy-start.13 = (s32[1,144]{1,0:T(1,128)S(1)}, s32[1,144]{1,0:T(1,128)}, u32[]{:S(2)}) copy-start(s32[1,144]{1,0:T(1,128)} %constant.32.clone.la_ref) | copy-start | bytes 1732
  26.9 0.7 %copy-start.14 = (s32[16]{0:T(128)S(1)}, s32[16]{0:T(128)}, u32[]{:S(2)}) copy-start(s32[16]{0:T(128)} %count_ref.1) | copy-start | bytes 196
  27.5 0.7 %copy-start.15 = (f32[6]{0:T(128)S(1)}, f32[6]{0:T(128)}, u32[]{:S(2)}) copy-start(f32[6]{0:T(128)} %param.42) | copy-start | bytes 76
  28.2 31.2 %copy-start.16 = (f32[3,96]{1,0:T(4,128)S(1)}, f32[3,96]{1,0:T(4,128)}, u32[]{:S(2)}) copy-start(f32[3,96]{1,0:T(4,128)} %param.32) | copy-start | bytes 3460
  51.7 4.3 %collective-permute-start.2 = (f32[3,24]{1,0:T(4,128)S(1)}, f32[3,24]{1,0:T(4,128)S(1)}, u32[]{:S(2)}, u32[]{:S(2)}) collective-permute-start(f32[3,24]{1,0:T(4,128)S(1)} %get-tuple-element.15), channel_id=1, source_target_pairs={{1,0},{2,1},{3,2},{4,3},{5,4},{6,5},{7,6},{8,7},{9,8},{10,9},{11,1... | collective-permute-start | bytes 872 | tf_op jit(solution)/shard_map/ppermute | solution.py:285
  53.6 5.8 %collective-permute-start.3 = (f32[3,24]{1,0:T(4,128)S(1)}, f32[3,24]{1,0:T(4,128)S(1)}, u32[]{:S(2)}, u32[]{:S(2)}) collective-permute-start(f32[3,24]{1,0:T(4,128)S(1)} %get-tuple-element.16), channel_id=1, source_target_pairs={{0,1},{1,2},{2,3},{3,4},{4,5},{5,6},{6,7},{7,8},{8,9},{9,10},{10,1... | collective-permute-start | bytes 872 | tf_op jit(solution)/shard_map/ppermute | solution.py:286

commit v2 on v1

v2 whole, which is shorter than its diff:
```python
import jax
import jax.numpy as jnp
from jax import lax
from jax.experimental import pallas as pl
from jax.experimental.pallas import tpu as pltpu
from jax.sharding import PartitionSpec as P

NSUB = 2
GROUP = 4
FIRST_VMEM = 60 << 20
SECOND_VMEM = 60 << 20
HIGHEST = lax.Precision.HIGHEST
BF = jnp.bfloat16
F32 = jnp.float32


def dot(x, y):
    return jnp.dot(x, y, preferred_element_type=F32)


def split(x):
    high = x.astype(BF)
    return high, (x - high.astype(F32)).astype(BF)


def turned(x, y, precision=None):
    dims = (((1,), (1,)), ((), ()))
    return lax.dot_general(x, y, dims, precision=precision, preferred_element_type=F32)


def upright(x, y, precision=None):
    dims = (((0,), (0,)), ((), ()))
    return lax.dot_general(x, y, dims, precision=precision, preferred_element_type=F32)


def iota(shape, dim):
    return lax.broadcasted_iota(jnp.int32, shape, dim)


def over(x, d):
    return (x * -(-65536 // d)) >> 16


def within(x, d):
    return x - over(x, d) * d


def where_one(mask):
    return jnp.where(mask, 1.0, 0.0).astype(BF)


def advance_rates(coef, wh_ref, points, width):
    half = width // 2

    def rates(stacked, columns, sub, rates_of, old_of, put):
        for jt in range(2):
            lo = jt * half
            if stacked is not None:
                pr = dot(stacked, wh_ref[:, lo : lo + half])
                pz = dot(stacked, wh_ref[:, width + lo : width + lo + half])
                pn = dot(stacked, wh_ref[:, 2 * width + lo : 2 * width + lo + half])
            for pt in range(points // 16):
                at = slice(pt * 16, pt * 16 + 16)
                ca, cb, cc, cr, cz = [coef[sub, i, at, lo : lo + half] for i in range(5)]
                for g in range(columns):
                    rows = slice(g * points + pt * 16, g * points + pt * 16 + 16)
                    vr = rates_of(g, lo)
                    vz = rates_of(g, width + lo)
                    vn = rates_of(g, 2 * width + lo)
                    if stacked is None:
                        new = cb * vr + cc * vz + ca * vn
                    else:
                        new = (
                            cb * (vr + pr[rows])
                            + cc * (vz + pz[rows])
                            + ca * (vn + cr * pn[rows])
                            + cz * old_of(g, at, lo).astype(F32)
                        )
                    put(g, at, lo, new)


    return rates


def point_terms(stacked, columns, points, wrep, wb):
    t = dot(stacked, wrep[...]).astype(BF).astype(F32)
    return [(t[g * points : (g + 1) * points] * wb[...]).astype(BF) for g in range(columns)]


def first(
    count_ref, disp_ref, load_ref, nodes_ref, bmat_ref, qw_ref, eps_ref, par_ref, hid_ref,
    wx_ref, wh_ref, bx_ref, bh_ref, wo_ref, bo_ref,
    res_ref, coef, gs, wb, wrep, b96, state_ref,
    d1, d2, onehot, mine_u, got_u, part, got_f, send_sem, recv_sem,
):
    peers = lax.axis_size("mesh")
    me = lax.axis_index("mesh")
    right, left = lax.rem(me + 1, peers), lax.rem(me + peers - 1, peers)
    barrier = pltpu.get_barrier_semaphore()
    for other in (left, right):
        pl.semaphore_signal(
            barrier, inc=1, device_id={"mesh": other}, device_id_type=pl.DeviceIdType.MESH
        )
    points, width = hid_ref.shape
    node_each, elems = nodes_ref.shape
    quads = points // elems
    strains = eps_ref.shape[0]
    param_count = par_ref.shape[0]
    owned = disp_ref.shape[1]
    halo = owned // 4
    span = node_each * 3
    wide = strains * span
    half = width // 2
    live = count_ref[me] * quads

    def send(src, dst, i, other):
        copy = pltpu.make_async_remote_copy(
            src_ref=src, dst_ref=dst, send_sem=send_sem.at[i], recv_sem=recv_sem.at[i],
            device_id={"mesh": other}, device_id_type=pl.DeviceIdType.MESH,
        )
        copy.start()
        return copy

    mine_u[...] = jnp.zeros_like(mine_u)
    mine_u[0:3, 0:owned] = disp_ref[...]
    pl.semaphore_wait(barrier, 2)
    to_right = send(mine_u, got_u.at[0], 0, right)
    to_left = send(mine_u, got_u.at[1], 1, left)

    alive = iota((points, 1), 0) < live
    by_elem = over(iota((points, elems), 0), quads) == iota((points, elems), 1)
    rep = where_one(by_elem)
    rep32 = jnp.where(by_elem, 1.0, 0.0)
    nodes = turned(rep32, nodes_ref[...].astype(F32), HIGHEST)
    weights = turned(rep32, qw_ref[...], HIGHEST)
    mine_q = within(iota((points, quads), 0), quads) == iota((points, quads), 1)
    weight = jnp.sum(jnp.where(mine_q, weights, 0.0), axis=1, keepdims=True)
    rows = dot(rep, bmat_ref[...])
    b = jnp.zeros((points, wide), F32)
    which = within(iota((points, 1), 0), quads)
    for q in range(quads):
        b += jnp.where(which == q, rows[:, q * wide : (q + 1) * wide], 0.0)
    b96[...] = b.astype(BF)
    wb[...] = jnp.where(alive, b * weight, 0.0)
    spread = where_one(over(iota((strains, wide), 1), span) == iota((strains, wide), 0))
    wrep[...] = upright(wo_ref[...].astype(BF), spread).astype(BF)
    nodes = jnp.where(
        nodes < halo,
        nodes + (owned - halo),
        jnp.where(nodes < halo + owned, nodes + (128 - halo), nodes + (256 - halo - owned)),
    )
    node = iota((points, 384), 1).astype(F32)
    for a in range(node_each):
        onehot[a * points : (a + 1) * points, :] = where_one(
            jnp.abs(nodes[:, a : a + 1] - node) < 0.5
        )
    material = upright(
        par_ref[...].astype(F32), wx_ref[strains : strains + param_count, :], HIGHEST
    ) + bx_ref[...].reshape(1, 3 * width)
    state = hid_ref[...]
    gh = dot(state, wh_ref[...])
    b_h = bh_ref[...].reshape(1, 3 * width)

    to_right.wait()
    to_left.wait()
    from_left = jnp.where(me > 0, 1.0, 0.0)
    from_right = jnp.where(me < peers - 1, 1.0, 0.0)
    u = jnp.concatenate([got_u[0] * from_left, mine_u[...], got_u[1] * from_right], axis=1)
    u_high, u_low = split(u)
    at_nodes = turned(onehot[...], jnp.concatenate([u_high, u_low], axis=0)).astype(BF)
    lane = within(iota((16, wide), 1), span)
    direction = where_one(within(lane, 3) == jnp.bitwise_and(iota((16, wide), 0), 7))
    values = dot(at_nodes, direction)
    which = over(within(iota((1, wide), 1), span), 3)
    mine = jnp.zeros((points, wide), F32)
    for a in range(node_each):
        mine += jnp.where(which == a, values[a * points : (a + 1) * points], 0.0)
    high, low = split(b * mine)
    strain = (turned(spread, high) + turned(spread, low)).astype(BF).astype(F32)
    eps = eps_ref[...].astype(F32)
    for sub in range(NSUB):
        fraction = (sub + 1.0) / NSUB
        drive = eps + fraction * (strain - eps)
        gx = material + upright(drive, wx_ref[0:strains, :], HIGHEST)
        if sub:
            gh = dot(state, wh_ref[...])
        gh = gh + b_h
        reset = jax.nn.sigmoid(gx[:, :width] + gh[:, :width])
        update = jax.nn.sigmoid(gx[:, width : 2 * width] + gh[:, width : 2 * width])
        cand_h = gh[:, 2 * width :]
        cand = jnp.tanh(gx[:, 2 * width :] + reset * cand_h)
        previous = state.astype(F32)
        ca = (1.0 - update) * (1.0 - cand * cand)
        coef[sub, 0] = ca
        coef[sub, 1] = ca * cand_h * (reset * (1.0 - reset))
        coef[sub, 2] = (previous - cand) * (update * (1.0 - update))
        coef[sub, 3] = reset
        coef[sub, 4] = update
        state = ((1.0 - update) * cand + update * previous).astype(BF)
    state_ref[...] = jnp.where(alive, state.astype(F32), 0.0).astype(BF)
    stress = dot(state, wrep[...]) + dot(bo_ref[...], spread.astype(F32))
    high, low = split(stress.astype(BF).astype(F32) * wb[...])
    shape = (node_each * 8, wide)
    lane = within(iota(shape, 1), span)
    node_row = iota(shape, 0)
    placed = where_one(over(lane, 3) * 8 + within(lane, 3) == node_row)
    by_point = turned(placed, high) + turned(placed, low)
    high, low = split(by_point)
    total = jnp.zeros((8, 384), F32)
    for a in range(node_each):
        hot = onehot[a * points : (a + 1) * points, :]
        total += dot(high[a * 8 : a * 8 + 8], hot) + dot(low[a * 8 : a * 8 + 8], hot)
    for i in range(3):
        part[i] = total[:, i * 128 : (i + 1) * 128]
    to_left = send(part.at[0], got_f.at[1], 2, left)
    to_right = send(part.at[2], got_f.at[0], 3, right)

    rates = advance_rates(coef, wh_ref, points, width)

    def strain_rate(scale):
        return lambda g, lane: wx_ref[g : g + 1, lane : lane + half] * scale

    def put(into):
        def store(g, at, lo, new):
            into[g * points + at.start : g * points + at.stop, lo : lo + half] = new.astype(BF)

        return store

    rates(None, strains, 0, strain_rate(1.0 / NSUB), None, put(d1))
    rates(
        d1[...], strains, 1, strain_rate(1.0),
        lambda g, at, lo: d1[g * points + at.start : g * points + at.stop, lo : lo + half],
        put(d2),
    )
    for i, piece in enumerate(point_terms(d2[...], strains, points, wrep, wb)):
        gs[i * points : (i + 1) * points, :] = piece
    to_left.wait()
    to_right.wait()
    force = part[1] + got_f[0] * from_left + got_f[1] * from_right
    res_ref[...] = load_ref[...] - force[0:3, 0:owned]


def second(
    count_ref, coef, gs, wb, wrep, b96, state_ref, wx_ref, wh_ref, sens_ref,
    stiff_ref, fs_ref, hn_ref, sn_ref,
    d1, d2, rsum,
):
    step = pl.program_id(0)
    last = pl.num_programs(0) - 1
    points, width = state_ref.shape
    elems = stiff_ref.shape[0]
    quads = points // elems
    strains = gs.shape[0] // points
    wide = wb.shape[1]
    span = wide // strains
    param_count = wx_ref.shape[0] - strains
    rows16 = rsum.shape[0] // param_count
    half = width // 2
    live = count_ref[lax.axis_index("mesh")] * quads
    total = where_one(over(iota((rows16, points), 1), quads) == iota((rows16, points), 0))
    rates = advance_rates(coef, wh_ref, points, width)

    def sens_rate(g, lane):
        return wx_ref[pl.ds(strains + step * GROUP + g, 1), lane : lane + half]

    def put_first(g, at, lo, new):
        d1[g * points + at.start : g * points + at.stop, lo : lo + half] = new.astype(BF)

    def put_last(g, at, lo, new):
        d2[g * points + at.start : g * points + at.stop, lo : lo + half] = new.astype(BF)
        alive = iota((16, 1), 0) + at.start < live
        sn_ref[at, g * width + lo : g * width + lo + half] = jnp.where(alive, new, 0.0).astype(BF)

    stacked = jnp.concatenate(
        [sens_ref[:, g * width : (g + 1) * width] for g in range(GROUP)], axis=0
    )
    rates(
        stacked, GROUP, 0, sens_rate,
        lambda g, at, lo: sens_ref[at, g * width + lo : g * width + lo + half], put_first,
    )
    rates(
        d1[...], GROUP, 1, sens_rate,
        lambda g, at, lo: d1[g * points + at.start : g * points + at.stop, lo : lo + half],
        put_last,
    )
    for g, piece in enumerate(point_terms(d2[...], GROUP, points, wrep, wb)):
        where = pl.multiple_of((step * GROUP + g) * rows16, rows16)
        rsum[pl.ds(where, rows16), :] = dot(total, piece).astype(BF)

    @pl.when(step == last)
    def _():
        hn_ref[...] = state_ref[...]
        b = b96[...].astype(F32)
        shape = (wide, span * span)
        ac, out = within(iota(shape, 0), span), iota(shape, 1)
        to_left = where_one(ac == over(out, span))
        to_right = where_one(ac == within(out, span))
        of = over(iota((1, wide), 1), span)
        acc = jnp.zeros((points, span * span), F32)
        for i in range(strains):
            one = jnp.where(of == i, b, 0.0).astype(BF)
            acc += dot(gs[i * points : (i + 1) * points, :], to_left) * dot(one, to_right)
        stiff_ref[...] = jnp.sum(acc.reshape(elems, quads, span * span), axis=1)
        shape = (wide, span * param_count)
        spread = where_one(within(iota(shape, 0), span) == over(iota(shape, 1), param_count))
        placed = dot(rsum[...], spread)
        fs = jnp.zeros((rows16, span * param_count), F32)
        of = within(iota((1, span * param_count), 1), param_count)
        for j in range(param_count):
            fs += jnp.where(of == j, placed[j * rows16 : (j + 1) * rows16], 0.0)
        fs_ref[...] = fs[:elems]


def on_device(
    elem_count, elem_nodes, bmat, quad_weight, displacement, load, eps_old, params,
    hidden, sens, w_x, w_h, b_x, b_h, w_out, b_out,
):
    elems, node_each = elem_nodes.shape
    points, strains = eps_old.shape
    param_count = params.shape[1]
    width = hidden.shape[1]
    span = node_each * 3
    wide = strains * span
    rows16 = -(-elems // 16) * 16
    smem = pl.BlockSpec(memory_space=pltpu.SMEM)
    vmem = pl.BlockSpec(memory_space=pltpu.VMEM)
    operands = [
        displacement, load, elem_nodes.T, bmat, quad_weight.T, eps_old.T, params.T, hidden,
        w_x, w_h, b_x, b_h, w_out.T, b_out[None],
    ]
    residual, coef, gs, wb, wrep, b96, state = pl.pallas_call(
        first,
        in_specs=[smem] + [vmem] * len(operands),
        out_specs=[vmem] * 7,
        out_shape=[
            jax.ShapeDtypeStruct(load.shape, F32),
            jax.ShapeDtypeStruct((NSUB, 5, points, width), F32),
            jax.ShapeDtypeStruct((strains * points, wide), BF),
            jax.ShapeDtypeStruct((points, wide), F32),
            jax.ShapeDtypeStruct((width, wide), BF),
            jax.ShapeDtypeStruct((points, wide), BF),
            jax.ShapeDtypeStruct((points, width), BF),
        ],
        scratch_shapes=[
            pltpu.VMEM((strains * points, width), BF),
            pltpu.VMEM((strains * points, width), BF),
            pltpu.VMEM((node_each * points, 384), BF),
            pltpu.VMEM((8, 128), F32),
            pltpu.VMEM((2, 8, 128), F32),
            pltpu.VMEM((3, 8, 128), F32),
            pltpu.VMEM((2, 8, 128), F32),
            pltpu.SemaphoreType.DMA((4,)),
            pltpu.SemaphoreType.DMA((4,)),
        ],
        compiler_params=pltpu.CompilerParams(
            vmem_limit_bytes=FIRST_VMEM, collective_id=0, has_side_effects=True
        ),
    )(elem_count, *operands)

    def whole(x):
        return pl.BlockSpec(x.shape, lambda i: (0,) * x.ndim)

    streamed = pl.BlockSpec((points, GROUP * width), lambda i: (0, i))
    outs = [
        jax.ShapeDtypeStruct((elems, span * span), F32),
        jax.ShapeDtypeStruct((elems, span * param_count), F32),
        jax.ShapeDtypeStruct((points, width), BF),
    ]
    operands = [coef, gs, wb, wrep, b96, state, w_x, w_h]
    stiffness, force_sens, hidden_next, sens_next = pl.pallas_call(
        second,
        grid=(param_count // GROUP,),
        in_specs=[smem] + [whole(x) for x in operands] + [streamed],
        out_specs=[whole(x) for x in outs] + [streamed],
        out_shape=outs + [jax.ShapeDtypeStruct(sens.shape, BF)],
        scratch_shapes=[
            pltpu.VMEM((GROUP * points, width), BF),
            pltpu.VMEM((GROUP * points, width), BF),
            pltpu.VMEM((param_count * rows16, wide), BF),
        ],
        compiler_params=pltpu.CompilerParams(vmem_limit_bytes=SECOND_VMEM),
    )(elem_count, *operands, sens)
    return (residual, stiffness, force_sens, hidden_next, sens_next)


def solution(mesh):
    both = ("groups", "mesh")
    rows, cols = P(both, None), P(None, both)
    return jax.shard_map(
        on_device,
        mesh=mesh,
        in_specs=(P("groups"), rows, rows, rows, cols, cols) + (rows,) * 4 + (P(),) * 6,
        out_specs=(cols, rows, rows, rows, rows),
        check_vma=False,
    )
```

time: 61.1 us -> 39.2 us (0.64)
  the two profiles are of different devices: /device:TPU:18 before, /device:TPU:0 now
where the time goes in v2:
time: 39.2 us; the launch traced here: 39.1 us
  Pallas kernels  37.8 us (96%)
  between operations  0.66 us (2%)
  local copies, waits for them, and re-layouts  0.58 us (1%)
    pallas_call x1, Pallas kernels, on_device(): pl.pallas_call(first, in_specs=[smem] + [vmem] * len(operands), out_specs...  19 us
    pallas_call x1, Pallas kernels, on_device(): pl.pallas_call(second, grid=(param_count // GROUP,), in_specs=[smem] + [w...  18.8 us

profile of v2, /device:TPU:0, one launch (start us, length us, event | category | flops | bytes accessed | tf_op | source)
XLA Modules:
  0.0 39.1 jit_solution(13891527915959325169)
XLA Ops:
  0.6 19.0 %shard_map.191 = (f32[3,96]{1,0:T(4,128)}, f32[2,5,96,512]{3,2,1,0:T(8,128)}, bf16[576,144]{1,0:T(8,128)(2,1)}, f32[96,144]{1,0:T(8,128)}, bf16[512,144]{1,0:T(8...) custom-call(s32[16]{0:T(128)} %count_ref.3, f32[3,96]{1,0:T(4,128)} %disp_ref.1, f32[3,96]{1,0:T(4,128)} %load_ref.1, ...), custom_call_target="tpu_custom_call" | custom-call | tf_op jit(solution)/shard_map/pallas_call | solution.py:331
  19.6 0.0 copy-start
  19.7 18.8 %shard_map.192 = (f32[12,576]{1,0:T(8,128)}, f32[12,768]{1,0:T(8,128)}, bf16[96,512]{1,0:T(8,128)(2,1)}, bf16[96,16384]{1,0:T(8,128)(2,1)}) custom-call(s32[16]{0:T(128)} %count_ref.3, f32[2,5,96,512]{3,2,1,0:T(8,128)} %get-tuple-element.17.coef, bf16[576,144]{1,0:T(8,128)(2,1)} %get-tuple-element.18.gs, f32[96,144]{1,0:T(8,128)} %get-tuple-element.19.wb, ...), custom_call_target="tpu_custom_call" | custom-call | tf_op jit(solution)/shard_map/pallas_call | solution.py:370
  38.5 0.0 copy-done
  38.5 0.6 %copy.22 = f32[3,96]{1,0:T(4,128)} copy(f32[3,96]{1,0:T(4,128)S(1)} %copy-done) | data formatting | bytes 2304
Async XLA Ops:
  19.6 18.8 %copy-start = (f32[3,96]{1,0:T(4,128)S(1)}, f32[3,96]{1,0:T(4,128)}, u32[]{:S(2)}) copy-start(f32[3,96]{1,0:T(4,128)} %get-tuple-element.32) | copy-start | bytes 3460
